TPU v7x, 32 devices: a whole 2x2x4 slice. The times are simulated.
32 devices in a mesh: shot: 2 (over x), dom: 8 (over z, y), sub: 2 (over core).
Axes of the slice: x: 2, y: 2, z: 4, core: 2. Of those that a mesh axis runs over, the one named last changes fastest.
Arguments:
- adjoint: float32 [4, 125, 16384], P(None, None, ('shot', 'dom', 'sub')), parts along dimension 2, may hold values from -6 to 6
- bulk: float32 [16384], P(('shot', 'dom', 'sub')), parts along dimension 0, may hold values from 0.5 to 2
- density: float32 [16384], P(('shot', 'dom', 'sub')), parts along dimension 0, may hold values from 0.5 to 2
- neighbours: int32 [6, 16384], P(None, ('shot', 'dom', 'sub')), parts along dimension 1, may hold values from 0 to 768, as said below
- keyframe: bfloat16 [4, 125, 16384], P(None, None, ('shot', 'dom', 'sub')), parts along dimension 2, may hold values from -6 to 6
- codes: int32 [4, 125, 16384], P(None, None, ('shot', 'dom', 'sub')), parts along dimension 2, may hold values from -127 to 127
- exponents: int32 [4, 16384], P(None, ('shot', 'dom', 'sub')), parts along dimension 1, may hold values from -8 to -6
- group_elem: int32 [16384], P(('shot', 'dom', 'sub')), parts along dimension 0, may hold values from 0 to 8191, as said below
Outputs:
- update: float32 [4, 125, 16384], P(None, None, ('shot', 'dom', 'sub')), parts along dimension 2
- image: float32 [2, 125, 16384], P(None, None, ('shot', 'dom', 'sub')), parts along dimension 2
There are 2 independent parts, one for each index of `shot`. A program takes and returns all parts, laid end to end along the dimension named above; each array names one. Nothing has to cross between parts.
Inputs may be any that keep to these rules, and one draw needn't show every extreme that they name: `neighbours`: block k holds element ids k * 512 onward; its elements are the cells of a 8 x 16 x 4 grid of unit cubes in an order of its own, cell (ix, iy, iz) with position j = ix * 16 + iy, and blocks are stacked along the third dimension in the order of k. Row f (faces -x, +x, -y, +y, -z, +z) gives the block-local index of the element across face f inside the block; for face -z of a bottom cell 512 + j, for face +z of a top cell 512 + 128 + j; 768 for faces on the block's x or y sides. Elements across a face share its nodes in the same order. `group_elem`: A permutation of all element ids. The rows of one block name at most 40 elements of any one block (ids k * 512 onward), and that many in every draw.
All inputs are finite; a program needn't handle non-finite values.
Results may differ from a plain program's by a relative error of at most 0.003.
Values may be sent and summed in bfloat16 or wider, within the bound.
A program may use at most 128 MiB of HBM per device.

v0:
```python
import functools

import jax
import jax.numpy as jnp
import numpy as np
from jax import lax
from jax.experimental import pallas as pl
from jax.experimental.pallas import tpu as pltpu
from jax.sharding import PartitionSpec as P

GX = 8
GY = 16
NODES = 125
FIELDS = 4
ORDER = 4
ROWS = 128
FROWS = 32

time_step = 0.04
lift_gain = 90.0 / 7.0

F32 = jnp.float32
BF16 = jnp.bfloat16
MESH = pl.DeviceIdType.MESH


def tables():
    points = np.linspace(-1.0, 1.0, 5)
    weights = np.ones(5)
    for i in range(5):
        for j in range(5):
            if i != j:
                weights[i] = weights[i] / (points[i] - points[j])
    slopes = np.zeros((5, 5))
    for i in range(5):
        for j in range(5):
            if i != j:
                slopes[i, j] = weights[j] / weights[i] / (points[i] - points[j])
        slopes[i, i] = -np.sum(slopes[i])
    whole = np.round(6.0 * slopes)
    eye = np.eye(5)
    ops = [
        np.kron(np.kron(whole, eye), eye),
        np.kron(np.kron(eye, whole), eye),
        np.kron(np.kron(eye, eye), whole),
    ]
    padded = [np.pad(op, ((0, 3), (0, 3))) for op in ops]
    grad = np.concatenate(padded, 0)
    grad = np.concatenate([grad, grad], 1)
    div = np.concatenate([padded[i // 2] for i in range(6)], 1)
    select = np.zeros((6 * FROWS, ROWS))
    grid = np.arange(NODES).reshape(5, 5, 5)
    for face in range(6):
        at = 0 if face % 2 == 0 else 4
        nodes = np.take(grid, at, axis=face // 2).reshape(25)
        select[face * FROWS + np.arange(25), nodes] = 1.0
    pick = np.concatenate([select, select], 1)
    place = np.concatenate([select.T, select.T], 1)
    place_rim = select.T[:, 4 * FROWS :]
    return tuple(jnp.asarray(m, BF16) for m in (grad, div, pick, place, place_rim))


def dot(a, b):
    return lax.dot_general(a, b, (((1,), (0,)), ((), ())), preferred_element_type=F32)


def split(value):
    high = value.astype(BF16)
    return high, (value - high.astype(F32)).astype(BF16)


def kernel(
    devices,
    subs,
    cap,
    adj_ref,
    bulk_ref,
    rho_ref,
    nb_ref,
    key_ref,
    code_ref,
    exp_ref,
    grp_ref,
    grad_ref,
    div_ref,
    pick_ref,
    place_ref,
    place_rim_ref,
    upd_ref,
    img_ref,
    dec_ref,
    hl_ref,
    acc_ref,
    w_ref,
    u_ref,
    j_ref,
    send_ref,
    recv_ref,
    rim_out,
    rim_in,
    send_sem,
    recv_sem,
    rim_send_sem,
    rim_recv_sem,
):
    elems = adj_ref.shape[2]
    rim = GX * GY
    me = lax.axis_index("dom") * subs + lax.axis_index("sub")

    def place_of(index):
        return {"dom": index // subs, "sub": index % subs}

    barrier = pltpu.get_barrier_semaphore()

    def greet(k, carry):
        other = lax.rem(me + k, devices)
        pl.semaphore_signal(barrier, inc=1, device_id=place_of(other), device_id_type=MESH)
        return carry

    lax.fori_loop(1, devices, greet, 0)

    group = grp_ref[...]
    owner = lax.div(group, jnp.int32(elems))
    ident = lax.rem(group, jnp.int32(elems)) + 1
    scale = jnp.exp2(exp_ref[...].astype(F32))
    for f in range(FIELDS):
        dec_ref[f, 0:NODES, :] = (
            key_ref[f].astype(F32) + code_ref[f].astype(F32) * scale[f : f + 1]
        )
        dec_ref[f, NODES:ROWS, :] = jnp.zeros((ROWS - NODES, elems), F32)
    dec_ref[0, NODES : NODES + 1, :] = lax.shift_right_logical(ident, 4).astype(F32)
    dec_ref[0, NODES + 1 : NODES + 2, :] = (ident & 15).astype(F32)
    decoded = dec_ref[...].astype(BF16).reshape(FIELDS * ROWS, elems)

    owned = lax.broadcasted_iota(jnp.int32, (devices, elems), 0) == owner
    owned_f = owned.astype(F32)
    before = (
        lax.broadcasted_iota(jnp.int32, (elems, elems), 0)
        < lax.broadcasted_iota(jnp.int32, (elems, elems), 1)
    )
    earlier = dot(owned_f.astype(BF16), before.astype(F32).astype(BF16))
    rank = jnp.sum(earlier * owned_f, axis=0, keepdims=True).astype(jnp.int32)
    slot = owner * cap + rank
    chosen = (lax.broadcasted_iota(jnp.int32, (devices * cap, elems), 0) == slot).astype(F32)
    outgoing = lax.dot_general(
        chosen.astype(BF16), decoded, (((1,), (1,)), ((), ())), preferred_element_type=F32
    )
    outgoing = jnp.concatenate(
        [outgoing[:, f * ROWS : (f + 1) * ROWS].reshape(devices, cap, ROWS) for f in range(FIELDS)],
        axis=1,
    )
    send_ref[...] = outgoing.astype(BF16)
    recv_ref[me] = send_ref[me]

    pl.semaphore_wait(barrier, devices - 1)

    def row_copy(k, landing):
        other = lax.rem(me + k, devices)
        return pltpu.make_async_remote_copy(
            src_ref=send_ref.at[other],
            dst_ref=recv_ref.at[landing(other)],
            send_sem=send_sem.at[k],
            recv_sem=recv_sem.at[landing(other)],
            device_id=place_of(other),
            device_id_type=MESH,
        )

    def start_rows(k, carry):
        row_copy(k, lambda other: me).start()
        return carry

    lax.fori_loop(1, devices, start_rows, 0)

    bulk = bulk_ref[...]
    inverse = 1.0 / rho_ref[...]

    def store_split(f, value):
        high, low = split(value)
        hl_ref[2 * f * ROWS : (2 * f + 1) * ROWS, :] = high
        hl_ref[(2 * f + 1) * ROWS : (2 * f + 2) * ROWS, :] = low

    def operator(gain):
        grad = dot(grad_ref[...], hl_ref[0 : 2 * ROWS, :])
        diverge = dot(div_ref[...], hl_ref[2 * ROWS :, :])
        by_bulk = bulk * (-gain / 3.0)
        by_rho = inverse * (-gain / 3.0)
        return [by_bulk * diverge] + [
            by_rho * grad[i * ROWS : (i + 1) * ROWS] for i in range(3)
        ]

    for f in range(FIELDS):
        acc_ref[f, 0:NODES, :] = adj_ref[f]
        acc_ref[f, NODES:ROWS, :] = jnp.zeros((ROWS - NODES, elems), F32)
    for f in range(FIELDS):
        store_split(f, acc_ref[f])
    for power in range(1, ORDER + 1):
        series = operator(time_step / (power + 1))
        for f in range(FIELDS):
            total = acc_ref[f] + series[f]
            acc_ref[f] = total
            store_split(f, total if power == ORDER else series[f])

    traces = [dot(pick_ref[...], hl_ref[2 * f * ROWS : (2 * f + 2) * ROWS, :]) for f in range(FIELDS)]
    half_bulk = 0.5 * bulk
    half_inverse = 0.5 * inverse
    for face in range(6):
        axis = face // 2
        sign = -1.0 if face % 2 == 0 else 1.0
        rows = [t[face * FROWS : (face + 1) * FROWS] for t in traces]
        flux_p = (sign * half_bulk) * rows[1 + axis]
        flux_v = (sign * half_inverse) * rows[0]
        for f in range(FIELDS):
            flux = flux_p if f == 0 else flux_v if f == 1 + axis else None
            given = rows[f] if flux is None else rows[f] + flux
            kept = rows[f] if flux is None else rows[f] - flux
            high, low = split(given)
            w_ref[face, f * FROWS : (f + 1) * FROWS, :] = high
            w_ref[face, ROWS + f * FROWS : ROWS + (f + 1) * FROWS, :] = low
            u_ref[face, f * FROWS : (f + 1) * FROWS, :] = kept

    rim_cell = lax.broadcasted_iota(jnp.int32, (rim, elems), 0)
    rim_hot = [
        (rim_cell + (elems + side * rim) == nb_ref[4 + side : 5 + side, :]).astype(F32).astype(BF16)
        for side in range(2)
    ]
    for side in range(2):
        rim_out[side] = lax.dot_general(
            w_ref[4 + side, 0:ROWS, :],
            rim_hot[side],
            (((1,), (1,)), ((), ())),
            preferred_element_type=F32,
        ).astype(BF16)

    def rim_copy(side, other):
        return pltpu.make_async_remote_copy(
            src_ref=rim_out.at[side],
            dst_ref=rim_in.at[1 - side],
            send_sem=rim_send_sem.at[side],
            recv_sem=rim_recv_sem.at[1 - side],
            device_id=place_of(other),
            device_id_type=MESH,
        )

    has_below = me > 0
    has_above = me < devices - 1

    @pl.when(has_below)
    def _():
        rim_copy(0, me - 1).start()

    @pl.when(has_above)
    def _():
        rim_copy(1, me + 1).start()

    @pl.when(me == 0)
    def _():
        rim_in[0] = jnp.zeros((ROWS, rim), BF16)

    @pl.when(me == devices - 1)
    def _():
        rim_in[1] = jnp.zeros((ROWS, rim), BF16)

    volume = operator(time_step)
    for f in range(FIELDS):
        upd_ref[f] = volume[f][0:NODES]

    cell = lax.broadcasted_iota(jnp.int32, (elems, elems), 0)
    for face in range(6):
        hot = (cell == nb_ref[face : face + 1, :]).astype(F32).astype(BF16)
        both = dot(w_ref[face ^ 1], hot)
        jump = both[0:ROWS] + both[ROWS:] - u_ref[face]
        for f in range(FIELDS):
            high, low = split(jump[f * FROWS : (f + 1) * FROWS])
            j_ref[f, face * FROWS : (face + 1) * FROWS, :] = high
            j_ref[f, (6 + face) * FROWS : (7 + face) * FROWS, :] = low
    for f in range(FIELDS):
        surface = dot(place_ref[...], j_ref[f])
        upd_ref[f] = upd_ref[f] + (time_step * lift_gain) * surface[0:NODES]

    @pl.when(has_above)
    def _():
        rim_copy(0, me + 1).wait_recv()

    @pl.when(has_below)
    def _():
        rim_copy(1, me - 1).wait_recv()

    outer = [dot(rim_in[side], rim_hot[side]).astype(BF16) for side in range(2)]
    for f in range(FIELDS):
        part = jnp.concatenate([o[f * FROWS : (f + 1) * FROWS] for o in outer], axis=0)
        surface = dot(place_rim_ref[...], part)
        upd_ref[f] = upd_ref[f] + (time_step * lift_gain) * surface[0:NODES]

    def wait_rows(k, carry):
        row_copy(k, lambda other: other).wait_recv()
        return carry

    lax.fori_loop(1, devices, wait_rows, 0)
    arrived = recv_ref[...].astype(F32)
    arrived = jnp.concatenate(
        [
            arrived[:, f * cap : (f + 1) * cap, :].reshape(devices * cap, ROWS)
            for f in range(FIELDS)
        ],
        axis=1,
    )
    target = arrived[:, NODES : NODES + 1] * 16.0 + arrived[:, NODES + 1 : NODES + 2] - 1.0
    hot = (
        lax.broadcasted_iota(jnp.int32, (devices * cap, elems), 1) == target.astype(jnp.int32)
    ).astype(F32)
    snapshot = lax.dot_general(
        arrived.astype(BF16),
        hot.astype(BF16),
        (((0,), (0,)), ((), ())),
        preferred_element_type=F32,
    )
    product = [snapshot[f * ROWS : (f + 1) * ROWS] * acc_ref[f] for f in range(FIELDS)]
    img_ref[0] = product[0][0:NODES]
    img_ref[1] = (product[1] + product[2] + product[3])[0:NODES]

    def wait_sent(k, carry):
        row_copy(k, lambda other: me).wait_send()
        return carry

    lax.fori_loop(1, devices, wait_sent, 0)

    @pl.when(has_below)
    def _():
        rim_copy(0, me - 1).wait_send()

    @pl.when(has_above)
    def _():
        rim_copy(1, me + 1).wait_send()


def local(adjoint, bulk, density, neighbours, keyframe, codes, exponents, group_elem):
    elems = adjoint.shape[2]
    devices = lax.axis_size(("dom", "sub"))
    subs = lax.axis_size("sub")
    rim = GX * GY
    mean = elems // devices
    cap = -(-(mean + mean // 4) // 8) * 8
    packed = FIELDS * cap
    vmem = pl.BlockSpec(memory_space=pltpu.VMEM)
    return pl.pallas_call(
        functools.partial(kernel, devices, subs, cap),
        out_shape=(
            jax.ShapeDtypeStruct((FIELDS, NODES, elems), F32),
            jax.ShapeDtypeStruct((2, NODES, elems), F32),
        ),
        in_specs=[vmem] * 13,
        out_specs=(vmem, vmem),
        scratch_shapes=[
            pltpu.VMEM((FIELDS, ROWS, elems), F32),
            pltpu.VMEM((2 * FIELDS * ROWS, elems), BF16),
            pltpu.VMEM((FIELDS, ROWS, elems), F32),
            pltpu.VMEM((6, 2 * ROWS, elems), BF16),
            pltpu.VMEM((6, ROWS, elems), F32),
            pltpu.VMEM((FIELDS, 12 * FROWS, elems), BF16),
            pltpu.VMEM((devices, packed, ROWS), BF16),
            pltpu.VMEM((devices, packed, ROWS), BF16),
            pltpu.VMEM((2, ROWS, rim), BF16),
            pltpu.VMEM((2, ROWS, rim), BF16),
            pltpu.SemaphoreType.DMA((devices,)),
            pltpu.SemaphoreType.DMA((devices,)),
            pltpu.SemaphoreType.DMA((2,)),
            pltpu.SemaphoreType.DMA((2,)),
        ],
        compiler_params=pltpu.CompilerParams(
            collective_id=0, has_side_effects=True, vmem_limit_bytes=48 * 1024 * 1024
        ),
    )(
        adjoint,
        bulk.reshape(1, elems),
        density.reshape(1, elems),
        neighbours,
        keyframe,
        codes,
        exponents,
        group_elem.reshape(1, elems),
        *tables(),
    )


def solution(mesh):
    placed = (
        P(None, None, ("shot", "dom", "sub")),
        P(("shot", "dom", "sub")),
        P(("shot", "dom", "sub")),
        P(None, ("shot", "dom", "sub")),
        P(None, None, ("shot", "dom", "sub")),
        P(None, None, ("shot", "dom", "sub")),
        P(None, ("shot", "dom", "sub")),
        P(("shot", "dom", "sub")),
    )
    return jax.shard_map(
        local,
        mesh=mesh,
        in_specs=placed,
        out_specs=(P(None, None, ("shot", "dom", "sub")), P(None, None, ("shot", "dom", "sub"))),
        check_vma=False,
    )
```

profile of v0, /device:TPU:13, one launch (start us, length us, event | category | flops | bytes accessed | tf_op | source)
XLA Modules:
  0.0 28.9 jit_solution(15859651207220953746)
XLA Ops:
  0.6 0.0 copy-start.10
  0.6 1.2 %copy.16.key_ref = bf16[4,125,512]{2,1,0:T(8,128)(2,1)S(1)} copy(bf16[4,125,512]{2,0,1:T(4,128)(2,1)} %param.17) | data formatting | bytes 1024000 | tf_op args[4]
  1.9 0.1 copy-done.10
  2.0 0.3 %copy.15.adj_ref = f32[4,125,512]{2,1,0:T(8,128)S(1)} copy(f32[4,125,512]{2,0,1:T(4,128)S(1)} %copy-done.10) | data formatting | bytes 2048000 | tf_op args[0]
  2.3 0.9 %copy-done.11 = s32[4,125,512]{2,0,1:T(4,128)S(1)} copy-done((s32[4,125,512]{2,0,1:T(4,128)S(1)}, s32[4,125,512]{2,0,1:T(4,128)}, u32[]{:S(2)}) %copy-start.11) | copy-done | bytes 1024024
  3.2 0.0 copy-start.4
  3.2 0.0 copy-start.5
  3.3 0.0 copy-start.6
  3.3 0.0 copy-start.7
  3.3 0.0 copy-start.8
  3.3 0.0 copy-start.9
  3.3 0.3 %copy.17.code_ref = s32[4,125,512]{2,1,0:T(8,128)S(1)} copy(s32[4,125,512]{2,0,1:T(4,128)S(1)} %copy-done.11) | data formatting | bytes 2048000 | tf_op args[5]
  3.6 0.5 %copy-done = bf16[128,768]{1,0:T(8,128)(2,1)S(1)} copy-done((bf16[128,768]{1,0:T(8,128)(2,1)S(1)}, bf16[128,768]{1,0:T(8,128)(2,1)}, u32[]{:S(2)}) %copy-start) | copy-done | bytes 196632
  4.1 0.1 copy-done.1
  4.2 0.1 copy-done.2
  4.3 0.0 copy-done.3
  4.3 0.0 copy-done.4
  4.4 0.0 copy-done.5
  4.4 0.0 copy-done.6
  4.4 0.0 copy-done.7
  4.4 0.0 copy-done.8
  4.4 21.7 %shard_map.140 = (f32[4,125,512]{2,1,0:T(8,128)S(1)}, f32[2,125,512]{2,1,0:T(8,128)S(1)}) custom-call(f32[4,125,512]{2,1,0:T(8,128)S(1)} %copy.15.adj_ref, f32[1,512]{1,0:T(1,128)S(1)} %bitcast.3, f32[1,512]{1,0:T(1,128)S(1)} %bitcast.4, s32[6,512]{1,0:T(8,128)S(1)} %copy-done.5, bf16[4,125,512]{2,1,0:T(8,128)(2,1)S(1)} %copy.16.key_ref, ...), custom_call_target="tpu_custom_call" | custom-call | tf_op jit(solution)/shard_map/pallas_call | solution.py:345
  26.1 1.6 %copy.18 = f32[4,125,512]{2,0,1:T(4,128)} copy(f32[4,125,512]{2,1,0:T(8,128)S(1)} %get-tuple-element.2) | data formatting | bytes 2048000 | tf_op jit(solution)/shard_map/pallas_call | solution.py:345
  27.7 1.2 %copy.19 = f32[2,125,512]{2,0,1:T(2,128)} copy(f32[2,125,512]{2,1,0:T(8,128)S(1)} %get-tuple-element.3) | data formatting | bytes 1024000 | tf_op jit(solution)/shard_map/pallas_call | solution.py:345
  (6 shorter events, 0.0 us)
Async XLA Ops:
  0.6 1.4 %copy-start.10 = (f32[4,125,512]{2,0,1:T(4,128)S(1)}, f32[4,125,512]{2,0,1:T(4,128)}, u32[]{:S(2)}) copy-start(f32[4,125,512]{2,0,1:T(4,128)} %param.13) | copy-start | bytes 3072004
  2.0 1.2 %copy-start.11 = (s32[4,125,512]{2,0,1:T(4,128)S(1)}, s32[4,125,512]{2,0,1:T(4,128)}, u32[]{:S(2)}) copy-start(s32[4,125,512]{2,0,1:T(4,128)} %param.18) | copy-start | bytes 3072004
  3.2 0.9 %copy-start = (bf16[128,768]{1,0:T(8,128)(2,1)S(1)}, bf16[128,768]{1,0:T(8,128)(2,1)}, u32[]{:S(2)}) copy-start(bf16[128,768]{1,0:T(8,128)(2,1)} %constant.11.clone.div_ref) | copy-start | bytes 589828
  3.2 1.0 %copy-start.1 = (bf16[384,256]{1,0:T(8,128)(2,1)S(1)}, bf16[384,256]{1,0:T(8,128)(2,1)}, u32[]{:S(2)}) copy-start(bf16[384,256]{1,0:T(8,128)(2,1)} %constant.10.clone.grad_ref) | copy-start | bytes 589828
  3.2 1.1 %copy-start.2 = (bf16[128,384]{1,0:T(8,128)(2,1)S(1)}, bf16[128,384]{1,0:T(8,128)(2,1)}, u32[]{:S(2)}) copy-start(bf16[128,384]{1,0:T(8,128)(2,1)} %constant.13.clone.place_ref) | copy-start | bytes 294916
  3.2 1.1 %copy-start.3 = (bf16[192,256]{1,0:T(8,128)(2,1)S(1)}, bf16[192,256]{1,0:T(8,128)(2,1)}, u32[]{:S(2)}) copy-start(bf16[192,256]{1,0:T(8,128)(2,1)} %constant.12.clone.pick_ref) | copy-start | bytes 294916
  3.2 1.1 %copy-start.4 = (bf16[128,64]{1,0:T(8,128)(2,1)S(1)}, bf16[128,64]{1,0:T(8,128)(2,1)}, u32[]{:S(2)}) copy-start(bf16[128,64]{1,0:T(8,128)(2,1)} %constant.14.clone.place_rim_ref) | copy-start | bytes 49156
  3.2 1.1 %copy-start.5 = (s32[6,512]{1,0:T(8,128)S(1)}, s32[6,512]{1,0:T(8,128)}, u32[]{:S(2)}) copy-start(s32[6,512]{1,0:T(8,128)} %nb_ref.1) | copy-start | bytes 36868
  3.3 1.1 %copy-start.6 = (s32[4,512]{1,0:T(4,128)S(1)}, s32[4,512]{1,0:T(4,128)}, u32[]{:S(2)}) copy-start(s32[4,512]{1,0:T(4,128)} %exp_ref.1) | copy-start | bytes 24580
  3.3 1.1 %copy-start.7 = (f32[512]{0:T(512)S(1)}, f32[512]{0:T(512)}, u32[]{:S(2)}) copy-start(f32[512]{0:T(512)} %param.14) | copy-start | bytes 6148
  3.3 1.1 %copy-start.8 = (f32[512]{0:T(512)S(1)}, f32[512]{0:T(512)}, u32[]{:S(2)}) copy-start(f32[512]{0:T(512)} %param.15) | copy-start | bytes 6148
  3.3 1.1 %copy-start.9 = (s32[512]{0:T(512)S(1)}, s32[512]{0:T(512)}, u32[]{:S(2)}) copy-start(s32[512]{0:T(512)} %param.20) | copy-start | bytes 6148
where the time goes:
time: 29.1 us; the launch traced here: 28.9 us
  Pallas kernels  21.7 us (75%)
  local copies, waits for them, and re-layouts  6.46 us (22%)
  between operations  0.73 us (3%)
    pallas_call x1, Pallas kernels, local(): pl.pallas_call(functools.partial(kernel, devices, subs, cap), out_shape=(...  21.7 us
    unnamed x27, local copies, waits for them, and re-layouts  3.66 us
    pallas_call x2, local copies, waits for them, and re-layouts, local(): pl.pallas_call(functools.partial(kernel, devices, subs, cap), out_shape=(...  2.8 us

commit v1 on v0

--- a/solution.py
+++ b/solution.py
@@ -47,7 +47,6 @@
     padded = [np.pad(op, ((0, 3), (0, 3))) for op in ops]
     grad = np.concatenate(padded, 0)
     grad = np.concatenate([grad, grad], 1)
-    div = np.concatenate([padded[i // 2] for i in range(6)], 1)
     select = np.zeros((6 * FROWS, ROWS))
     grid = np.arange(NODES).reshape(5, 5, 5)
     for face in range(6):
@@ -55,9 +54,8 @@
         nodes = np.take(grid, at, axis=face // 2).reshape(25)
         select[face * FROWS + np.arange(25), nodes] = 1.0
     pick = np.concatenate([select, select], 1)
-    place = np.concatenate([select.T, select.T], 1)
-    place_rim = select.T[:, 4 * FROWS :]
-    return tuple(jnp.asarray(m, BF16) for m in (grad, div, pick, place, place_rim))
+    place = np.concatenate([select.T, select.T[:, 4 * FROWS :]], 1)
+    return jnp.asarray(np.concatenate([grad, pick, place], 0), BF16)
 
 
 def dot(a, b):
@@ -73,24 +71,19 @@
     devices,
     subs,
     cap,
-    adj_ref,
     bulk_ref,
     rho_ref,
     nb_ref,
-    key_ref,
-    code_ref,
-    exp_ref,
     grp_ref,
-    grad_ref,
-    div_ref,
-    pick_ref,
-    place_ref,
-    place_rim_ref,
+    coded_ref,
+    adj_ref,
+    table_ref,
     upd_ref,
     img_ref,
     dec_ref,
     hl_ref,
     acc_ref,
+    sum_ref,
     w_ref,
     u_ref,
     j_ref,
@@ -105,7 +98,10 @@
 ):
     elems = adj_ref.shape[2]
     rim = GX * GY
+    half = devices // 2
     me = lax.axis_index("dom") * subs + lax.axis_index("sub")
+    my_base = (me // half) * half
+    far_base = half - my_base
 
     def place_of(index):
         return {"dom": index // subs, "sub": index % subs}
@@ -122,16 +118,6 @@
     group = grp_ref[...]
     owner = lax.div(group, jnp.int32(elems))
     ident = lax.rem(group, jnp.int32(elems)) + 1
-    scale = jnp.exp2(exp_ref[...].astype(F32))
-    for f in range(FIELDS):
-        dec_ref[f, 0:NODES, :] = (
-            key_ref[f].astype(F32) + code_ref[f].astype(F32) * scale[f : f + 1]
-        )
-        dec_ref[f, NODES:ROWS, :] = jnp.zeros((ROWS - NODES, elems), F32)
-    dec_ref[0, NODES : NODES + 1, :] = lax.shift_right_logical(ident, 4).astype(F32)
-    dec_ref[0, NODES + 1 : NODES + 2, :] = (ident & 15).astype(F32)
-    decoded = dec_ref[...].astype(BF16).reshape(FIELDS * ROWS, elems)
-
     owned = lax.broadcasted_iota(jnp.int32, (devices, elems), 0) == owner
     owned_f = owned.astype(F32)
     before = (
@@ -141,35 +127,54 @@
     earlier = dot(owned_f.astype(BF16), before.astype(F32).astype(BF16))
     rank = jnp.sum(earlier * owned_f, axis=0, keepdims=True).astype(jnp.int32)
     slot = owner * cap + rank
-    chosen = (lax.broadcasted_iota(jnp.int32, (devices * cap, elems), 0) == slot).astype(F32)
-    outgoing = lax.dot_general(
-        chosen.astype(BF16), decoded, (((1,), (1,)), ((), ())), preferred_element_type=F32
-    )
-    outgoing = jnp.concatenate(
-        [outgoing[:, f * ROWS : (f + 1) * ROWS].reshape(devices, cap, ROWS) for f in range(FIELDS)],
-        axis=1,
-    )
-    send_ref[...] = outgoing.astype(BF16)
-    recv_ref[me] = send_ref[me]
-
-    pl.semaphore_wait(barrier, devices - 1)
-
-    def row_copy(k, landing):
-        other = lax.rem(me + k, devices)
+
+    dec_ref[:, 0:NODES, :] = jnp.swapaxes(coded_ref[...].astype(F32), 0, 1)
+    for f in range(FIELDS):
+        dec_ref[f, NODES:ROWS, :] = jnp.zeros((ROWS - NODES, elems), F32)
+    dec_ref[0, NODES : NODES + 1, :] = lax.shift_right_logical(ident, 4).astype(F32)
+    dec_ref[0, NODES + 1 : NODES + 2, :] = (ident & 15).astype(F32)
+    decoded = dec_ref[...].astype(BF16).reshape(FIELDS * ROWS, elems)
+
+    def dispatch(base):
+        cell = lax.broadcasted_iota(jnp.int32, (half * cap, elems), 0) + base * cap
+        rows = lax.dot_general(
+            (cell == slot).astype(F32).astype(BF16),
+            decoded,
+            (((1,), (1,)), ((), ())),
+            preferred_element_type=F32,
+        )
+        rows = jnp.concatenate(
+            [rows[:, f * ROWS : (f + 1) * ROWS].reshape(half, cap, ROWS) for f in range(FIELDS)],
+            axis=1,
+        )
+        send_ref[pl.ds(base, half)] = rows.astype(BF16)
+
+    def far(k):
+        return far_base + lax.rem(me + k, half)
+
+    def near(k):
+        return my_base + lax.rem(me + k, half)
+
+    def row_copy(other, landing):
         return pltpu.make_async_remote_copy(
             src_ref=send_ref.at[other],
-            dst_ref=recv_ref.at[landing(other)],
-            send_sem=send_sem.at[k],
-            recv_sem=recv_sem.at[landing(other)],
+            dst_ref=recv_ref.at[landing],
+            send_sem=send_sem.at[other],
+            recv_sem=recv_sem.at[landing],
             device_id=place_of(other),
             device_id_type=MESH,
         )
 
     def start_rows(k, carry):
-        row_copy(k, lambda other: me).start()
+        row_copy(lax.rem(me + k, devices), me).start()
         return carry
 
-    lax.fori_loop(1, devices, start_rows, 0)
+    dispatch(far_base)
+    dispatch(my_base)
+    pl.semaphore_wait(barrier, devices - 1)
+    ahead = (5 * devices) // 8
+    lax.fori_loop(1, ahead, start_rows, 0)
+    recv_ref[me] = send_ref[me]
 
     bulk = bulk_ref[...]
     inverse = 1.0 / rho_ref[...]
@@ -180,16 +185,22 @@
         hl_ref[(2 * f + 1) * ROWS : (2 * f + 2) * ROWS, :] = low
 
     def operator(gain):
-        grad = dot(grad_ref[...], hl_ref[0 : 2 * ROWS, :])
-        diverge = dot(div_ref[...], hl_ref[2 * ROWS :, :])
+        grad = dot(table_ref[0 : 3 * ROWS, :], hl_ref[0 : 2 * ROWS, :])
+        diverge = sum(
+            dot(
+                table_ref[i * ROWS : (i + 1) * ROWS, :],
+                hl_ref[2 * (i + 1) * ROWS : 2 * (i + 2) * ROWS, :],
+            )
+            for i in range(3)
+        )
         by_bulk = bulk * (-gain / 3.0)
         by_rho = inverse * (-gain / 3.0)
         return [by_bulk * diverge] + [
             by_rho * grad[i * ROWS : (i + 1) * ROWS] for i in range(3)
         ]
 
-    for f in range(FIELDS):
-        acc_ref[f, 0:NODES, :] = adj_ref[f]
+    acc_ref[:, 0:NODES, :] = jnp.swapaxes(adj_ref[...], 0, 1)
+    for f in range(FIELDS):
         acc_ref[f, NODES:ROWS, :] = jnp.zeros((ROWS - NODES, elems), F32)
     for f in range(FIELDS):
         store_split(f, acc_ref[f])
@@ -200,7 +211,9 @@
             acc_ref[f] = total
             store_split(f, total if power == ORDER else series[f])
 
-    traces = [dot(pick_ref[...], hl_ref[2 * f * ROWS : (2 * f + 2) * ROWS, :]) for f in range(FIELDS)]
+    pick = table_ref[3 * ROWS : 3 * ROWS + 6 * FROWS, :]
+    place = table_ref[3 * ROWS + 6 * FROWS :, :]
+    traces = [dot(pick, hl_ref[2 * f * ROWS : (2 * f + 2) * ROWS, :]) for f in range(FIELDS)]
     half_bulk = 0.5 * bulk
     half_inverse = 0.5 * inverse
     for face in range(6):
@@ -252,6 +265,8 @@
     def _():
         rim_copy(1, me + 1).start()
 
+    lax.fori_loop(ahead, devices, start_rows, 0)
+
     @pl.when(me == 0)
     def _():
         rim_in[0] = jnp.zeros((ROWS, rim), BF16)
@@ -262,7 +277,7 @@
 
     volume = operator(time_step)
     for f in range(FIELDS):
-        upd_ref[f] = volume[f][0:NODES]
+        sum_ref[f] = volume[f]
 
     cell = lax.broadcasted_iota(jnp.int32, (elems, elems), 0)
     for face in range(6):
@@ -272,10 +287,11 @@
         for f in range(FIELDS):
             high, low = split(jump[f * FROWS : (f + 1) * FROWS])
             j_ref[f, face * FROWS : (face + 1) * FROWS, :] = high
-            j_ref[f, (6 + face) * FROWS : (7 + face) * FROWS, :] = low
-    for f in range(FIELDS):
-        surface = dot(place_ref[...], j_ref[f])
-        upd_ref[f] = upd_ref[f] + (time_step * lift_gain) * surface[0:NODES]
+            j_ref[f, (8 + face) * FROWS : (9 + face) * FROWS, :] = low
+    for f in range(FIELDS):
+        sum_ref[f] = sum_ref[f] + (time_step * lift_gain) * dot(
+            place[:, 0 : 6 * FROWS], j_ref[f, 8 * FROWS : 14 * FROWS, :]
+        )
 
     @pl.when(has_above)
     def _():
@@ -287,39 +303,58 @@
 
     outer = [dot(rim_in[side], rim_hot[side]).astype(BF16) for side in range(2)]
     for f in range(FIELDS):
-        part = jnp.concatenate([o[f * FROWS : (f + 1) * FROWS] for o in outer], axis=0)
-        surface = dot(place_rim_ref[...], part)
-        upd_ref[f] = upd_ref[f] + (time_step * lift_gain) * surface[0:NODES]
-
-    def wait_rows(k, carry):
-        row_copy(k, lambda other: other).wait_recv()
+        for side in range(2):
+            j_ref[f, (6 + side) * FROWS : (7 + side) * FROWS, :] = outer[side][
+                f * FROWS : (f + 1) * FROWS
+            ]
+        sum_ref[f] = sum_ref[f] + (time_step * lift_gain) * dot(
+            place, j_ref[f, 0 : 8 * FROWS, :]
+        )
+    upd_ref[...] = jnp.swapaxes(sum_ref[:, 0:NODES, :], 0, 1)
+
+    def scatter(base):
+        arrived = recv_ref[pl.ds(base, half)].astype(F32)
+        arrived = jnp.concatenate(
+            [
+                arrived[:, f * cap : (f + 1) * cap, :].reshape(half * cap, ROWS)
+                for f in range(FIELDS)
+            ],
+            axis=1,
+        )
+        target = arrived[:, NODES : NODES + 1] * 16.0 + arrived[:, NODES + 1 : NODES + 2] - 1.0
+        hot = (
+            lax.broadcasted_iota(jnp.int32, (half * cap, elems), 1) == target.astype(jnp.int32)
+        ).astype(F32)
+        return lax.dot_general(
+            arrived.astype(BF16),
+            hot.astype(BF16),
+            (((0,), (0,)), ((), ())),
+            preferred_element_type=F32,
+        )
+
+    def wait_near(k, carry):
+        other = near(k)
+        row_copy(other, other).wait_recv()
         return carry
 
-    lax.fori_loop(1, devices, wait_rows, 0)
-    arrived = recv_ref[...].astype(F32)
-    arrived = jnp.concatenate(
-        [
-            arrived[:, f * cap : (f + 1) * cap, :].reshape(devices * cap, ROWS)
-            for f in range(FIELDS)
-        ],
-        axis=1,
-    )
-    target = arrived[:, NODES : NODES + 1] * 16.0 + arrived[:, NODES + 1 : NODES + 2] - 1.0
-    hot = (
-        lax.broadcasted_iota(jnp.int32, (devices * cap, elems), 1) == target.astype(jnp.int32)
-    ).astype(F32)
-    snapshot = lax.dot_general(
-        arrived.astype(BF16),
-        hot.astype(BF16),
-        (((0,), (0,)), ((), ())),
-        preferred_element_type=F32,
-    )
-    product = [snapshot[f * ROWS : (f + 1) * ROWS] * acc_ref[f] for f in range(FIELDS)]
-    img_ref[0] = product[0][0:NODES]
-    img_ref[1] = (product[1] + product[2] + product[3])[0:NODES]
+    def wait_far(k, carry):
+        other = far(k)
+        row_copy(other, other).wait_recv()
+        return carry
+
+    lax.fori_loop(1, half, wait_near, 0)
+    dec_ref[...] = scatter(my_base).reshape(FIELDS, ROWS, elems)
+    lax.fori_loop(0, half, wait_far, 0)
+    snapshot = scatter(far_base)
+    product = [
+        (snapshot[f * ROWS : (f + 1) * ROWS] + dec_ref[f]) * acc_ref[f] for f in range(FIELDS)
+    ]
+    image = jnp.stack([product[0], product[1] + product[2] + product[3]], axis=0)
+    img_ref[...] = jnp.swapaxes(image[:, 0:NODES, :], 0, 1)
 
     def wait_sent(k, carry):
-        row_copy(k, lambda other: me).wait_send()
+        other = lax.rem(me + k, devices)
+        row_copy(other, me).wait_send()
         return carry
 
     lax.fori_loop(1, devices, wait_sent, 0)
@@ -342,21 +377,25 @@
     cap = -(-(mean + mean // 4) // 8) * 8
     packed = FIELDS * cap
     vmem = pl.BlockSpec(memory_space=pltpu.VMEM)
-    return pl.pallas_call(
+    shift = jnp.maximum(exponents[:, None, :], codes - 256) + 8
+    delta = lax.shift_left(codes, shift)
+    coded = (keyframe.astype(F32) + delta.astype(F32) * 2.0**-8).astype(BF16)
+    update, image = pl.pallas_call(
         functools.partial(kernel, devices, subs, cap),
         out_shape=(
-            jax.ShapeDtypeStruct((FIELDS, NODES, elems), F32),
-            jax.ShapeDtypeStruct((2, NODES, elems), F32),
+            jax.ShapeDtypeStruct((NODES, FIELDS, elems), F32),
+            jax.ShapeDtypeStruct((NODES, 2, elems), F32),
         ),
-        in_specs=[vmem] * 13,
+        in_specs=[vmem] * 7,
         out_specs=(vmem, vmem),
         scratch_shapes=[
             pltpu.VMEM((FIELDS, ROWS, elems), F32),
             pltpu.VMEM((2 * FIELDS * ROWS, elems), BF16),
             pltpu.VMEM((FIELDS, ROWS, elems), F32),
+            pltpu.VMEM((FIELDS, ROWS, elems), F32),
             pltpu.VMEM((6, 2 * ROWS, elems), BF16),
             pltpu.VMEM((6, ROWS, elems), F32),
-            pltpu.VMEM((FIELDS, 12 * FROWS, elems), BF16),
+            pltpu.VMEM((FIELDS, 14 * FROWS, elems), BF16),
             pltpu.VMEM((devices, packed, ROWS), BF16),
             pltpu.VMEM((devices, packed, ROWS), BF16),
             pltpu.VMEM((2, ROWS, rim), BF16),
@@ -367,19 +406,18 @@
             pltpu.SemaphoreType.DMA((2,)),
         ],
         compiler_params=pltpu.CompilerParams(
-            collective_id=0, has_side_effects=True, vmem_limit_bytes=48 * 1024 * 1024
+            collective_id=0, has_side_effects=True, vmem_limit_bytes=40 * 1024 * 1024
         ),
     )(
-        adjoint,
         bulk.reshape(1, elems),
         density.reshape(1, elems),
         neighbours,
-        keyframe,
-        codes,
-        exponents,
         group_elem.reshape(1, elems),
-        *tables(),
+        jnp.swapaxes(coded, 0, 1),
+        jnp.swapaxes(adjoint, 0, 1),
+        tables(),
     )
+    return jnp.swapaxes(update, 0, 1), jnp.swapaxes(image, 0, 1)
 
 
 def solution(mesh):

time: 29.1 us -> 26.9 us (0.924)
  the two profiles are of different devices: /device:TPU:13 before, /device:TPU:18 now
where the time goes in v1:
time: 26.9 us; the launch traced here: 26.8 us
  Pallas kernels  22.1 us (82%)
  other arithmetic  2.12 us (8%)
  local copies, waits for them, and re-layouts  1.77 us (7%)
  between operations  0.74 us (3%)
    pallas_call x1, Pallas kernels, local(): pl.pallas_call(functools.partial(kernel, devices, subs, cap), out_shape=(...  22.1 us
    transpose x1, other arithmetic, local(): jnp.swapaxes(coded, 0, 1)  2.12 us
    unnamed x14, local copies, waits for them, and re-layouts  1.77 us

profile of v1, /device:TPU:18, one launch (start us, length us, event | category | flops | bytes accessed | tf_op | source)
XLA Modules:
  0.0 26.8 jit_solution(18113528808482472357)
XLA Ops:
  0.6 0.0 copy-start
  0.6 0.0 copy-start.1
  0.7 0.0 copy-start.2
  0.7 0.0 copy-start.3
  0.7 0.0 copy-start.4
  0.7 0.0 copy-start.5
  0.7 2.1 %fusion.coded_ref = bf16[125,4,512]{2,1,0:T(4,128)(2,1)S(1)} fusion(s32[4,125,512]{2,0,1:T(4,128)} %param.14, s32[4,512]{1,0:T(4,128)} %param.15, bf16[4,125,512]{2,0,1:T(4,128)(2,1)} %param.13), kind=kLoop, calls=%fused_computation.1 | loop fusion | flops 2304000 | bytes 2056192 | tf_op jit(solution)/shard_map/transpose | solution.py:416
  2.8 0.0 copy-done
  2.8 0.0 copy-done.1
  2.8 0.0 copy-done.2
  2.9 0.0 copy-done.3
  2.9 0.0 copy-done.4
  2.9 0.0 copy-done.5
  2.9 22.1 %shard_map.104 = (f32[125,4,512]{2,1,0:T(4,128)S(1)}, f32[125,2,512]{2,1,0:T(2,128)S(1)}) custom-call(f32[1,512]{1,0:T(1,128)S(1)} %bitcast.11, f32[1,512]{1,0:T(1,128)S(1)} %bitcast.12, s32[6,512]{1,0:T(8,128)S(1)} %copy-done.2, s32[1,512]{1,0:T(1,128)S(1)} %bitcast.13, bf16[125,4,512]{2,1,0:T(4,128)(2,1)S(1)} %fusion.coded_ref, ...), custom_call_target="tpu_custom_call" | custom-call | tf_op jit(solution)/shard_map/pallas_call | solution.py:383
  25.0 1.0 %copy.13 = f32[4,125,512]{2,0,1:T(4,128)} copy(f32[4,125,512]{2,0,1:T(4,128)S(1)} %bitcast.9) | data formatting | bytes 2048000
  26.0 0.8 %copy.14 = f32[2,125,512]{2,0,1:T(2,128)} copy(f32[2,125,512]{2,0,1:T(2,128)S(1)} %bitcast.10) | data formatting | bytes 1024000
Async XLA Ops:
  0.6 2.2 %copy-start = (f32[4,125,512]{2,0,1:T(4,128)S(1)}, f32[4,125,512]{2,0,1:T(4,128)}, u32[]{:S(2)}) copy-start(f32[4,125,512]{2,0,1:T(4,128)} %param.9) | copy-start | bytes 3072004
  0.6 2.2 %copy-start.1 = (bf16[704,256]{1,0:T(8,128)(2,1)S(1)}, bf16[704,256]{1,0:T(8,128)(2,1)}, u32[]{:S(2)}) copy-start(bf16[704,256]{1,0:T(8,128)(2,1)} %constant.9.clone.table_ref) | copy-start | bytes 1081348
  0.7 2.2 %copy-start.2 = (s32[6,512]{1,0:T(8,128)S(1)}, s32[6,512]{1,0:T(8,128)}, u32[]{:S(2)}) copy-start(s32[6,512]{1,0:T(8,128)} %nb_ref.1) | copy-start | bytes 36868
  0.7 2.2 %copy-start.3 = (f32[512]{0:T(512)S(1)}, f32[512]{0:T(512)}, u32[]{:S(2)}) copy-start(f32[512]{0:T(512)} %param.10) | copy-start | bytes 6148
  0.7 2.2 %copy-start.4 = (f32[512]{0:T(512)S(1)}, f32[512]{0:T(512)}, u32[]{:S(2)}) copy-start(f32[512]{0:T(512)} %param.11) | copy-start | bytes 6148
  0.7 2.2 %copy-start.5 = (s32[512]{0:T(512)S(1)}, s32[512]{0:T(512)}, u32[]{:S(2)}) copy-start(s32[512]{0:T(512)} %param.16) | copy-start | bytes 6148

commit v2 on v1

--- a/solution.py
+++ b/solution.py
@@ -172,7 +172,7 @@
     dispatch(far_base)
     dispatch(my_base)
     pl.semaphore_wait(barrier, devices - 1)
-    ahead = (5 * devices) // 8
+    ahead = devices // 2
     lax.fori_loop(1, ahead, start_rows, 0)
     recv_ref[me] = send_ref[me]
 
@@ -293,25 +293,6 @@
             place[:, 0 : 6 * FROWS], j_ref[f, 8 * FROWS : 14 * FROWS, :]
         )
 
-    @pl.when(has_above)
-    def _():
-        rim_copy(0, me + 1).wait_recv()
-
-    @pl.when(has_below)
-    def _():
-        rim_copy(1, me - 1).wait_recv()
-
-    outer = [dot(rim_in[side], rim_hot[side]).astype(BF16) for side in range(2)]
-    for f in range(FIELDS):
-        for side in range(2):
-            j_ref[f, (6 + side) * FROWS : (7 + side) * FROWS, :] = outer[side][
-                f * FROWS : (f + 1) * FROWS
-            ]
-        sum_ref[f] = sum_ref[f] + (time_step * lift_gain) * dot(
-            place, j_ref[f, 0 : 8 * FROWS, :]
-        )
-    upd_ref[...] = jnp.swapaxes(sum_ref[:, 0:NODES, :], 0, 1)
-
     def scatter(base):
         arrived = recv_ref[pl.ds(base, half)].astype(F32)
         arrived = jnp.concatenate(
@@ -344,6 +325,25 @@
 
     lax.fori_loop(1, half, wait_near, 0)
     dec_ref[...] = scatter(my_base).reshape(FIELDS, ROWS, elems)
+    @pl.when(has_above)
+    def _():
+        rim_copy(0, me + 1).wait_recv()
+
+    @pl.when(has_below)
+    def _():
+        rim_copy(1, me - 1).wait_recv()
+
+    outer = [dot(rim_in[side], rim_hot[side]).astype(BF16) for side in range(2)]
+    for f in range(FIELDS):
+        for side in range(2):
+            j_ref[f, (6 + side) * FROWS : (7 + side) * FROWS, :] = outer[side][
+                f * FROWS : (f + 1) * FROWS
+            ]
+        sum_ref[f] = sum_ref[f] + (time_step * lift_gain) * dot(
+            place, j_ref[f, 0 : 8 * FROWS, :]
+        )
+    upd_ref[...] = jnp.swapaxes(sum_ref[:, 0:NODES, :], 0, 1)
+
     lax.fori_loop(0, half, wait_far, 0)
     snapshot = scatter(far_base)
     product = [

time: 26.9 us -> 25.8 us (0.959)
  the two profiles are of different devices: /device:TPU:18 before, /device:TPU:13 now
where the time goes in v2:
time: 25.8 us; the launch traced here: 25.6 us
  Pallas kernels  21 us (81%)
  other arithmetic  2.12 us (8%)
  local copies, waits for them, and re-layouts  1.77 us (7%)
  between operations  0.74 us (3%)
    pallas_call x1, Pallas kernels, local(): pl.pallas_call(functools.partial(kernel, devices, subs, cap), out_shape=(...  21 us
    transpose x1, other arithmetic, local(): jnp.swapaxes(coded, 0, 1)  2.12 us
    unnamed x14, local copies, waits for them, and re-layouts  1.77 us

profile of v2, /device:TPU:13, one launch (start us, length us, event | category | flops | bytes accessed | tf_op | source)
XLA Modules:
  0.0 25.6 jit_solution(6283875081435143205)
XLA Ops:
  0.6 0.0 copy-start
  0.6 0.0 copy-start.1
  0.7 0.0 copy-start.2
  0.7 0.0 copy-start.3
  0.7 0.0 copy-start.4
  0.7 0.0 copy-start.5
  0.7 2.1 %fusion.coded_ref = bf16[125,4,512]{2,1,0:T(4,128)(2,1)S(1)} fusion(s32[4,125,512]{2,0,1:T(4,128)} %param.14, s32[4,512]{1,0:T(4,128)} %param.15, bf16[4,125,512]{2,0,1:T(4,128)(2,1)} %param.13), kind=kLoop, calls=%fused_computation.1 | loop fusion | flops 2304000 | bytes 2056192 | tf_op jit(solution)/shard_map/transpose | solution.py:416
  2.8 0.0 copy-done
  2.8 0.0 copy-done.1
  2.8 0.0 copy-done.2
  2.9 0.0 copy-done.3
  2.9 0.0 copy-done.4
  2.9 0.0 copy-done.5
  2.9 21.0 %shard_map.104 = (f32[125,4,512]{2,1,0:T(4,128)S(1)}, f32[125,2,512]{2,1,0:T(2,128)S(1)}) custom-call(f32[1,512]{1,0:T(1,128)S(1)} %bitcast.11, f32[1,512]{1,0:T(1,128)S(1)} %bitcast.12, s32[6,512]{1,0:T(8,128)S(1)} %copy-done.2, s32[1,512]{1,0:T(1,128)S(1)} %bitcast.13, bf16[125,4,512]{2,1,0:T(4,128)(2,1)S(1)} %fusion.coded_ref, ...), custom_call_target="tpu_custom_call" | custom-call | tf_op jit(solution)/shard_map/pallas_call | solution.py:383
  23.9 1.0 %copy.13 = f32[4,125,512]{2,0,1:T(4,128)} copy(f32[4,125,512]{2,0,1:T(4,128)S(1)} %bitcast.9) | data formatting | bytes 2048000
  24.8 0.8 %copy.14 = f32[2,125,512]{2,0,1:T(2,128)} copy(f32[2,125,512]{2,0,1:T(2,128)S(1)} %bitcast.10) | data formatting | bytes 1024000
Async XLA Ops:
  0.6 2.2 %copy-start = (f32[4,125,512]{2,0,1:T(4,128)S(1)}, f32[4,125,512]{2,0,1:T(4,128)}, u32[]{:S(2)}) copy-start(f32[4,125,512]{2,0,1:T(4,128)} %param.9) | copy-start | bytes 3072004
  0.6 2.2 %copy-start.1 = (bf16[704,256]{1,0:T(8,128)(2,1)S(1)}, bf16[704,256]{1,0:T(8,128)(2,1)}, u32[]{:S(2)}) copy-start(bf16[704,256]{1,0:T(8,128)(2,1)} %constant.9.clone.table_ref) | copy-start | bytes 1081348
  0.7 2.2 %copy-start.2 = (s32[6,512]{1,0:T(8,128)S(1)}, s32[6,512]{1,0:T(8,128)}, u32[]{:S(2)}) copy-start(s32[6,512]{1,0:T(8,128)} %nb_ref.1) | copy-start | bytes 36868
  0.7 2.2 %copy-start.3 = (f32[512]{0:T(512)S(1)}, f32[512]{0:T(512)}, u32[]{:S(2)}) copy-start(f32[512]{0:T(512)} %param.10) | copy-start | bytes 6148
  0.7 2.2 %copy-start.4 = (f32[512]{0:T(512)S(1)}, f32[512]{0:T(512)}, u32[]{:S(2)}) copy-start(f32[512]{0:T(512)} %param.11) | copy-start | bytes 6148
  0.7 2.2 %copy-start.5 = (s32[512]{0:T(512)S(1)}, s32[512]{0:T(512)}, u32[]{:S(2)}) copy-start(s32[512]{0:T(512)} %param.16) | copy-start | bytes 6148
